TPU v7x, 32 devices: a whole 2x2x4 slice. The times are simulated.
32 devices in a mesh: groups: 2 (over y), dp: 4 (over z), mp: 2 (over x), sub: 2 (over core).
Axes of the slice: x: 2, y: 2, z: 4, core: 2. Of those that a mesh axis runs over, the one named last changes fastest.
Arguments:
- example_blocks: int32 [32], P(('groups', 'dp')), parts along dimension 0, may hold values from 1 to 19, as said below
- layer_input: bfloat16 [4224, 4096], P(('groups', 'dp'), ('mp', 'sub')), parts along dimension 0, may hold values from -6 to 6
- out_grad: bfloat16 [4224, 4096], P(('groups', 'dp'), ('mp', 'sub')), parts along dimension 0, may hold values from -6 to 6
- gate_pre: bfloat16 [4224, 14336], P(('groups', 'dp'), ('mp', 'sub')), parts along dimension 0, may hold values from -6 to 6
- up_pre: bfloat16 [4224, 14336], P(('groups', 'dp'), ('mp', 'sub')), parts along dimension 0, may hold values from -6 to 6
- down_weight: bfloat16 [14336, 4096], P(('mp', 'sub'), 'dp'), may hold values from -0.046875 to 0.046875
- proj_input: bfloat16 [4096, 64], P(('mp', 'sub')), may hold values from -0.09375 to 0.09375
- proj_output: bfloat16 [4096, 64], P(('mp', 'sub')), may hold values from -0.09375 to 0.09375
- proj_hidden: bfloat16 [14336, 64], P(('mp', 'sub')), may hold values from -0.046875 to 0.046875
- proj_gate: bfloat16 [14336, 64], P(('mp', 'sub')), may hold values from -0.046875 to 0.046875
- proj_up: bfloat16 [14336, 64], P(('mp', 'sub')), may hold values from -0.046875 to 0.046875
Outputs:
- proj_grads: float32 [32, 12288], P(('groups', 'dp'), ('mp', 'sub')), parts along dimension 0
There are 2 independent parts, one for each index of `groups`. A program takes and returns all parts, laid end to end along the dimension named above; an argument that names none is the same for every part. Nothing has to cross between parts.
Inputs may be any that keep to these rules, and one draw needn't show every extreme that they name: `example_blocks`: the entries of one data shard's 4 examples sum to at most 22, exactly 22 on some shard, and all entries together sum to exactly 13 times the number of data shards.
All inputs are finite; a program needn't handle non-finite values.
Results may differ from a plain program's by a relative error of at most 0.0041.
Values may be sent and summed in bfloat16 or wider, within the bound.
A program may use at most 128 MiB of HBM per device.

v0:
```python
import jax
import jax.numpy as jnp
from jax import lax
from jax.sharding import PartitionSpec as P

BLK = 24


def example_sums(example_blocks, home_proj, hidden_proj, gate_proj, up_proj):
    rows, rank_dim = hidden_proj.shape
    num_examples = example_blocks.shape[0]
    block_ends = jnp.cumsum(example_blocks) * BLK
    row_ids = jnp.arange(rows, dtype=jnp.int32)
    row_example = jnp.sum(
        (row_ids[:, None] >= block_ends[None, :]).astype(jnp.int32), axis=1, dtype=jnp.int32
    )
    labels = jnp.arange(num_examples, dtype=jnp.int32)
    selector = (row_example[:, None] == labels[None, :]).astype(jnp.float32)
    input_side = home_proj[:, :rank_dim].astype(jnp.float32)
    output_side = home_proj[:, rank_dim:].astype(jnp.float32)

    def spread(left):
        return (selector[:, :, None] * left[:, None, :]).reshape(rows, num_examples * rank_dim)

    def outer(left, right):
        return lax.dot_general(
            left, right, (((0,), (0,)), ((), ())), precision=lax.Precision.HIGHEST
        ).reshape(num_examples, rank_dim, -1)

    down_part = outer(spread(hidden_proj), output_side)
    both = outer(spread(input_side), jnp.concatenate([gate_proj, up_proj], axis=1))
    parts = [down_part, both[:, :, :rank_dim], both[:, :, rank_dim:]]
    summed = jnp.concatenate([p.reshape(num_examples, rank_dim * rank_dim) for p in parts], axis=1)
    return lax.psum_scatter(summed, ("mp", "sub"), scatter_dimension=1, tiled=True)


def home_projections(layer_input, out_grad, proj_input, proj_output):
    home_proj = jnp.concatenate(
        [
            jnp.dot(layer_input, proj_input, preferred_element_type=jnp.float32),
            jnp.dot(out_grad, proj_output, preferred_element_type=jnp.float32),
        ],
        axis=1,
    )
    return lax.psum(home_proj, ("mp", "sub")).astype(jnp.bfloat16)


def body(
    example_blocks,
    layer_input,
    out_grad,
    gate_pre,
    up_pre,
    down_weight,
    proj_input,
    proj_output,
    proj_hidden,
    proj_gate,
    proj_up,
):
    ff_cols = gate_pre.shape[1]
    half = ff_cols // 2
    full_grads = lax.all_gather(out_grad, ("mp", "sub"), axis=1, tiled=True)
    mine = lax.dynamic_slice_in_dim(down_weight, lax.axis_index("groups") * half, half, 0)
    weight_half = lax.all_gather(mine, "dp", axis=1, tiled=True)
    weight = lax.all_gather(weight_half, "groups", axis=0, tiled=True)
    home_proj = home_projections(layer_input, out_grad, proj_input, proj_output)
    hidden_grad = lax.dot_general(
        full_grads, weight, (((1,), (1,)), ((), ())), preferred_element_type=jnp.float32
    )
    gate_val = gate_pre.astype(jnp.float32)
    up_val = up_pre.astype(jnp.float32)
    sigmoid_gate = jax.nn.sigmoid(gate_val)
    hidden = (gate_val * sigmoid_gate * up_val).astype(jnp.bfloat16)
    gate_grad = (
        hidden_grad * up_val * sigmoid_gate * (1.0 + gate_val * (1.0 - sigmoid_gate))
    ).astype(jnp.bfloat16)
    up_grad = (hidden_grad * gate_val * sigmoid_gate).astype(jnp.bfloat16)
    hidden_proj = jnp.dot(hidden, proj_hidden, preferred_element_type=jnp.float32)
    gate_proj = jnp.dot(gate_grad, proj_gate, preferred_element_type=jnp.float32)
    up_proj = jnp.dot(up_grad, proj_up, preferred_element_type=jnp.float32)
    return example_sums(example_blocks, home_proj, hidden_proj, gate_proj, up_proj)


def solution(mesh):
    rows = P(("groups", "dp"), ("mp", "sub"))
    proj = P(("mp", "sub"), None)
    placed = (P(("groups", "dp")),) + (rows,) * 4 + (P(("mp", "sub"), "dp"),) + (proj,) * 5
    return jax.shard_map(
        body, mesh=mesh, in_specs=placed, out_specs=rows, check_vma=False
    )
```

profile of v0, /device:TPU:0, one launch (start us, length us, event | category | flops | bytes accessed | tf_op | source)
XLA Modules:
  0.0 757.3 jit_solution(8109193607790649638)
XLA Ops:
  6.5 0.0 copy-start
  6.5 0.0 all-gather.4.cloned.1.call-start
  6.5 4.3 constant_dynamic-slice_fusion
  10.8 0.0 all-gather.4.cloned.1.call-update
  10.9 0.0 all-gather.8.cloned.1.call-start
  10.9 0.7 all-gather.8.cloned.1.call-update
  11.6 0.0 copy-start.2
  11.6 0.0 copy-start.3
  11.7 0.0 all-gather.6.cloned.1.call-start
  11.7 254.5 %all-gather.4.cloned.1.call-done = bf16[1792,4096]{1,0:T(8,128)(2,1)} async-done(((bf16[1792,1024]{1,0:T(8,128)(2,1)}), bf16[1792,4096]{1,0:T(8,128)(2,1)}) %all-gather.4.cloned.1.call-update) | async-done | bytes 14680080 | tf_op jit(solution)/shard_map/all_gather | solution.py:65
  266.2 0.0 copy-start.4
  266.2 0.0 copy-start.10
  266.2 0.0 copy-start.7
  266.2 0.0 all-gather.6.cloned.1.call-update
  266.3 0.0 reduce-scatter.4.cloned.1.call-start
  266.3 0.0 copy-done.2
  266.3 0.0 copy-done.3
  266.3 0.5 fusion.32
  266.8 0.0 copy-done
  266.8 0.3 copy-done.4
  267.1 0.5 fusion.31
  267.6 0.0 copy-done.10
  267.7 0.2 reduce-window.8
  267.8 0.1 convert_reduce_fusion
  267.9 0.0 copy-done.7
  268.0 5.6 fusion.10
  273.6 21.0 %all-reduce.1 = bf16[528,128]{0,1:T(8,128)(2,1)S(1)} all-reduce(f32[528,128]{0,1:T(8,128)S(1)} %pad_maximum_fusion), channel_id=1, replica_groups=mesh['groups'=2,'dp'=4,'mp'=2,'sub'=2] {'mp','sub'}, use_global_device_ids=true, to_apply=%region_2.3 | all-reduce | flops 67584 | bytes 405504 | tf_op jit(solution)/shard_map/psum | solution.py:45
  294.7 0.4 fusion.23
  295.1 0.1 reshape_reshape.3
  295.2 0.0 copy-start.8
  295.3 11.2 %all-gather.8.cloned.1.call-done = bf16[528,4096]{1,0:T(8,128)(2,1)} async-done(((bf16[528,1024]{1,0:T(8,128)(2,1)}), bf16[528,4096]{1,0:T(8,128)(2,1)}) %all-gather.8.cloned.1.call-update) | async-done | bytes 4325392 | tf_op jit(solution)/shard_map/all_gather | solution.py:63
  306.5 343.6 %all-gather.6.cloned.1.call-done = bf16[3584,4096]{1,0:T(8,128)(2,1)} async-done(((bf16[1792,4096]{1,0:T(8,128)(2,1)}), bf16[3584,4096]{1,0:T(8,128)(2,1)}) %all-gather.6.cloned.1.call-update) | async-done | bytes 29360144 | tf_op jit(solution)/shard_map/all_gather | solution.py:66
  650.1 0.0 copy-start.5
  650.1 24.5 %fusion.33 = f32[3584,528]{0,1:T(8,128)} fusion(bf16[3584,4096]{1,0:T(8,128)(2,1)} %all-gather.6.cloned.1.call-done, bf16[528,4096]{1,0:T(8,128)(2,1)} %all-gather.8.cloned.1.call-done), kind=kOutput, calls=%fused_computation.46 | convolution fusion | flops 15502147584 | bytes 41254912 | tf_op jit(solution)/shard_map/dot_general | solution.py:68
  674.7 0.0 copy-done.8
  674.7 0.0 copy-done.5
  674.7 0.0 copy-start.6
  674.7 0.0 copy-start.9
  674.7 0.0 copy-start.11
  674.7 5.6 fusion.12
  680.3 0.0 copy-done.6
  680.3 0.0 copy-done.9
  680.3 1.0 copy-done.11
  681.3 3.3 fusion.14
  684.6 0.7 fusion.16
  685.3 0.1 fusion.30
  685.4 0.0 copy-start.1
  685.4 0.1 reshape.68
  685.5 0.1 reshape.69
  685.7 4.0 copy.20
  689.7 0.0 reduce-scatter.4.cloned.1.call-update
  689.7 58.5 %reduce-scatter.4.cloned.1.call-done = f32[3072,4]{1,0:T(8,128)} async-done(((f32[12288,4]{1,0:T(8,128)}), f32[3072,4]{1,0:T(8,128)}) %reduce-scatter.4.cloned.1.call-update) | async-done | bytes 49168
  748.2 2.5 copy.21
  750.7 0.0 copy-done.1
  (6 shorter events, 0.1 us)
Async XLA Ops:
  6.5 260.3 %copy-start = (bf16[528,1024]{1,0:T(8,128)(2,1)S(1)}, bf16[528,1024]{1,0:T(8,128)(2,1)}, u32[]{:S(2)}) copy-start(bf16[528,1024]{1,0:T(8,128)(2,1)} %param.12) | copy-start | bytes 3244036
  6.5 259.7 %all-gather.4.cloned.1.call-start = ((), (), s32[]{:S(2)}) async-start(), calls=%async_computation.1 | async-start | bytes 18350080 | tf_op jit(solution)/shard_map/all_gather | solution.py:65
  10.9 295.6 %all-gather.8.cloned.1.call-start = ((), (), s32[]{:S(2)}) async-start(), calls=%async_computation.3 | async-start | bytes 5406720 | tf_op jit(solution)/shard_map/all_gather | solution.py:63
  11.6 254.7 %copy-start.2 = (bf16[528,1024]{1,0:T(8,128)(2,1)S(1)}, bf16[528,1024]{1,0:T(8,128)(2,1)}, u32[]{:S(2)}) copy-start(bf16[528,1024]{1,0:T(8,128)(2,1)} %param.13) | copy-start | bytes 3244036
  11.6 254.7 %copy-start.3 = (bf16[1024,64]{0,1:T(8,128)(2,1)S(1)}, bf16[1024,64]{0,1:T(8,128)(2,1)}, u32[]{:S(2)}) copy-start(bf16[1024,64]{0,1:T(8,128)(2,1)} %param.18) | copy-start | bytes 393220
  11.7 638.5 %all-gather.6.cloned.1.call-start = ((), (), s32[]{:S(2)}) async-start(), calls=%async_computation.2 | async-start | bytes 44040192 | tf_op jit(solution)/shard_map/all_gather | solution.py:66
  266.2 0.9 copy-start.4
  266.2 1.4 copy-start.10
  266.2 1.7 copy-start.7
  266.3 482.0 %reduce-scatter.4.cloned.1.call-start = ((), (), s32[]{:S(2)}) async-start(), calls=%async_computation.4 | async-start | bytes 7864320
  295.2 379.4 %copy-start.8 = (bf16[3584,64]{0,1:T(8,128)(2,1)S(1)}, bf16[3584,64]{0,1:T(8,128)(2,1)}, u32[]{:S(2)}) copy-start(bf16[3584,64]{0,1:T(8,128)(2,1)} %param.21) | copy-start | bytes 1376260
  650.1 24.5 %copy-start.5 = (bf16[528,3584]{1,0:T(8,128)(2,1)S(1)}, bf16[528,3584]{1,0:T(8,128)(2,1)}, u32[]{:S(2)}) copy-start(bf16[528,3584]{1,0:T(8,128)(2,1)} %param.14) | copy-start | bytes 11354116
  674.7 5.6 copy-start.6
  674.7 5.6 copy-start.9
  674.7 6.6 copy-start.11
  685.4 65.3 %copy-start.1 = (bf16[528,1024]{1,0:T(8,128)(2,1)S(1)}, bf16[528,1024]{1,0:T(8,128)(2,1)}, u32[]{:S(2)}) copy-start(bf16[528,1024]{1,0:T(8,128)(2,1)} %param.12) | copy-start | bytes 3244036
Sparse Core Ops, SparseCore 0:
  11.0 255.1 all-gather.3
  267.8 38.6 all-gather.7
  308.1 342.0 all-gather.5
  689.8 58.3 reduce-scatter.3
where the time goes:
time: 757 us
  waiting for transfers between devices  669 us (88%)
  matrix products  41.2 us (5%)
  blocking collectives  21 us (3%)
  between operations  13.4 us (2%)
  local copies, waits for them, and re-layouts  12.5 us (2%)
    all_gather x1, waiting for transfers between devices, body(): weight = lax.all_gather(weight_half, 'groups', axis=0, tiled=True)  344 us
    all_gather x1, waiting for transfers between devices, body(): weight_half = lax.all_gather(mine, 'dp', axis=1, tiled=True)  255 us
    unnamed x5, waiting for transfers between devices  59.3 us
    dot_general x1, matrix products, body(): lax.dot_general(full_grads, weight, (((1,), (1,)), ((), ())), preferred_e...  24.5 us
    psum x1, blocking collectives, home_projections(): return lax.psum(home_proj, ('mp', 'sub')).astype(jnp.bfloat16)  21 us
  transfers between devices with their start and end apart: 4, of which 4 were waited for; matrix products, arithmetic and copies ran while one was open for 1% of the time, Pallas kernels for 0%

commit v1 on v0

--- a/solution.py
+++ b/solution.py
@@ -1,9 +1,263 @@
+import functools
+
 import jax
 import jax.numpy as jnp
 from jax import lax
+from jax.experimental import pallas as pl
+from jax.experimental.pallas import tpu as pltpu
 from jax.sharding import PartitionSpec as P
 
 BLK = 24
+CHUNK = 256
+MESH = pl.DeviceIdType.MESH
+
+
+def gather_kernel(
+    shards,
+    feature_shards,
+    cores,
+    chunks,
+    grads_ref,
+    gate_ref,
+    up_ref,
+    weight_ref,
+    proj_hidden_ref,
+    proj_gate_ref,
+    proj_up_ref,
+    hidden_out,
+    gate_out,
+    up_out,
+    weights,
+    grads,
+    grad_send,
+    grad_recv,
+    local_sem,
+    send_right,
+    send_left,
+    recv_sem,
+    group_send,
+    group_recv,
+):
+    group = lax.axis_index("groups")
+    here = lax.axis_index("dp")
+    feature = lax.axis_index("mp") * cores + lax.axis_index("sub")
+    half = chunks * CHUNK
+    has_left = here > 0
+    has_right = here < shards - 1
+
+    def rows_of(group_at, chunk):
+        return pl.ds(pl.multiple_of(group_at * half + chunk * CHUNK, CHUNK), CHUNK)
+
+    def grad_copy(to, origin):
+        return pltpu.make_async_remote_copy(
+            src_ref=grads_ref,
+            dst_ref=grads.at[origin],
+            send_sem=grad_send.at[to],
+            recv_sem=grad_recv.at[origin],
+            device_id={"mp": to // cores, "sub": to % cores},
+            device_id_type=MESH,
+        )
+
+    def line_copy(source_ref, origin, chunk, to, sems):
+        return pltpu.make_async_remote_copy(
+            src_ref=source_ref,
+            dst_ref=weights.at[origin, rows_of(group, chunk)],
+            send_sem=sems.at[origin, chunk],
+            recv_sem=recv_sem.at[origin, chunk],
+            device_id={"dp": to},
+            device_id_type=MESH,
+        )
+
+    def group_copy(group_at, origin, chunk):
+        block = weights.at[origin, rows_of(group_at, chunk)]
+        return pltpu.make_async_remote_copy(
+            src_ref=block,
+            dst_ref=block,
+            send_sem=group_send.at[origin, chunk],
+            recv_sem=group_recv.at[origin, chunk],
+            device_id={"groups": 1 - group},
+            device_id_type=MESH,
+        )
+
+    def held(origin, chunk):
+        return weights.at[origin, rows_of(group, chunk)]
+
+    barrier = pltpu.get_barrier_semaphore()
+    pl.semaphore_signal(barrier, inc=1, device_id={"groups": 1 - group}, device_id_type=MESH)
+    for step in range(1, feature_shards):
+        to = lax.rem(feature + step, feature_shards)
+        pl.semaphore_signal(
+            barrier, inc=1, device_id={"mp": to // cores, "sub": to % cores}, device_id_type=MESH
+        )
+
+    @pl.when(has_left)
+    def _():
+        pl.semaphore_signal(barrier, inc=1, device_id={"dp": here - 1}, device_id_type=MESH)
+
+    @pl.when(has_right)
+    def _():
+        pl.semaphore_signal(barrier, inc=1, device_id={"dp": here + 1}, device_id_type=MESH)
+
+    at_an_end = jnp.logical_or(here == 0, here == shards - 1)
+
+    @pl.when(at_an_end)
+    def _():
+        pl.semaphore_wait(barrier, feature_shards + 1)
+
+    @pl.when(jnp.logical_not(at_an_end))
+    def _():
+        pl.semaphore_wait(barrier, feature_shards + 2)
+
+    def send_own(chunk):
+        own = weight_ref.at[rows_of(group, chunk)]
+
+        @pl.when(has_right)
+        def _():
+            line_copy(own, here, chunk, here + 1, send_right).start()
+
+        @pl.when(has_left)
+        def _():
+            line_copy(own, here, chunk, here - 1, send_left).start()
+
+    send_own(0)
+    for step in range(1, feature_shards):
+        grad_copy(lax.rem(feature + step, feature_shards), feature).start()
+    local_grads = pltpu.make_async_copy(grads_ref, grads.at[feature], local_sem.at[0])
+    local_grads.start()
+    local_weight = pltpu.make_async_copy(weight_ref, weights.at[here], local_sem.at[1])
+    local_weight.start()
+    hidden_out[...] = jnp.zeros_like(hidden_out)
+    gate_out[...] = jnp.zeros_like(gate_out)
+    up_out[...] = jnp.zeros_like(up_out)
+    local_grads.wait()
+    local_weight.wait()
+
+    def pass_on(origin, chunk, more, to, sems):
+        line_copy(held(origin, chunk), origin, chunk, to, sems).wait_recv()
+
+        @pl.when(more)
+        def _():
+            line_copy(held(origin, chunk), origin, chunk, to, sems).start()
+
+        group_copy(group, origin, chunk).start()
+
+    def work(group_at, chunk):
+        span = rows_of(group_at, chunk)
+        hidden_grad = jnp.zeros((grads_ref.shape[0], CHUNK), jnp.float32)
+        for origin in range(shards):
+            hidden_grad += lax.dot_general(
+                grads[origin],
+                weights[origin, span, :],
+                (((1,), (1,)), ((), ())),
+                preferred_element_type=jnp.float32,
+            )
+        gate_val = gate_ref[:, span].astype(jnp.float32)
+        up_val = up_ref[:, span].astype(jnp.float32)
+        sigmoid_gate = jax.nn.sigmoid(gate_val)
+        silu_gate = gate_val * sigmoid_gate
+        hidden = (silu_gate * up_val).astype(jnp.bfloat16)
+        gate_grad = (
+            hidden_grad * up_val * sigmoid_gate * (1.0 + gate_val * (1.0 - sigmoid_gate))
+        ).astype(jnp.bfloat16)
+        up_grad = (hidden_grad * silu_gate).astype(jnp.bfloat16)
+        hidden_out[...] += jnp.dot(
+            hidden, proj_hidden_ref[span, :], preferred_element_type=jnp.float32
+        )
+        gate_out[...] += jnp.dot(
+            gate_grad, proj_gate_ref[span, :], preferred_element_type=jnp.float32
+        )
+        up_out[...] += jnp.dot(up_grad, proj_up_ref[span, :], preferred_element_type=jnp.float32)
+
+    def tick(at, carry):
+        @pl.when(at + 1 < chunks)
+        def _():
+            send_own(at + 1)
+
+        for step in range(1, shards):
+            chunk = at - step
+            inside = jnp.logical_and(chunk >= 0, chunk < chunks)
+
+            @pl.when(jnp.logical_and(inside, here >= step))
+            def _():
+                pass_on(here - step, chunk, has_right, here + 1, send_right)
+
+            @pl.when(jnp.logical_and(inside, here + step < shards))
+            def _():
+                pass_on(here + step, chunk, has_left, here - 1, send_left)
+
+        @pl.when(at == shards - 1)
+        def _():
+            for step in range(1, feature_shards):
+                origin = lax.rem(feature + step, feature_shards)
+                grad_copy(origin, origin).wait_recv()
+
+        @pl.when(at >= shards)
+        def _():
+            for step in range(1, shards):
+                group_copy(1 - group, lax.rem(here + step, shards), at - shards).wait_recv()
+            work(1 - group, at - shards)
+
+        @pl.when(jnp.logical_and(at >= shards - 1, at < chunks + shards - 1))
+        def _():
+            work(group, at - shards + 1)
+
+        return carry
+
+    lax.fori_loop(0, chunks + shards, tick, 0)
+
+    for step in range(1, feature_shards):
+        grad_copy(lax.rem(feature + step, feature_shards), feature).wait_send()
+
+    def drain(chunk, carry):
+        for origin in range(shards):
+            @pl.when(jnp.logical_and(has_right, here >= origin))
+            def _():
+                line_copy(held(origin, chunk), origin, chunk, here + 1, send_right).wait_send()
+
+            @pl.when(jnp.logical_and(has_left, here <= origin))
+            def _():
+                line_copy(held(origin, chunk), origin, chunk, here - 1, send_left).wait_send()
+
+            @pl.when(here != origin)
+            def _():
+                group_copy(group, origin, chunk).wait_send()
+
+        return carry
+
+    lax.fori_loop(0, chunks, drain, 0)
+
+
+def gathered_projections(
+    shards, feature_shards, cores, out_grad, gate_pre, up_pre, down_weight, proj_hidden, proj_gate, proj_up
+):
+    rows, columns = out_grad.shape
+    ff_cols = gate_pre.shape[1]
+    rank_dim = proj_hidden.shape[1]
+    chunks = ff_cols // (2 * CHUNK)
+    in_vmem = pl.BlockSpec(memory_space=pltpu.VMEM)
+    full = columns * feature_shards
+    return pl.pallas_call(
+        functools.partial(gather_kernel, shards, feature_shards, cores, chunks),
+        out_shape=[jax.ShapeDtypeStruct((rows, rank_dim), jnp.float32)] * 3,
+        in_specs=[in_vmem] * 3 + [pl.BlockSpec(memory_space=pl.ANY)] + [in_vmem] * 3,
+        out_specs=[in_vmem] * 3,
+        scratch_shapes=[
+            pltpu.VMEM((shards, ff_cols, columns), jnp.bfloat16),
+            pltpu.VMEM((feature_shards, rows, columns), jnp.bfloat16),
+            pltpu.SemaphoreType.DMA((feature_shards,)),
+            pltpu.SemaphoreType.DMA((feature_shards,)),
+            pltpu.SemaphoreType.DMA((2,)),
+        ]
+        + [pltpu.SemaphoreType.DMA((shards, chunks))] * 5,
+        compiler_params=pltpu.CompilerParams(
+            collective_id=0, has_side_effects=True, vmem_limit_bytes=60 * 2**20
+        ),
+        cost_estimate=pl.CostEstimate(
+            flops=2 * rows * ff_cols * (full + 3 * rank_dim),
+            bytes_accessed=2 * ff_cols * (2 * rows + full),
+            transcendentals=rows * ff_cols,
+        ),
+    )(out_grad, gate_pre, up_pre, down_weight, proj_hidden, proj_gate, proj_up)
 
 
 def example_sums(example_blocks, home_proj, hidden_proj, gate_proj, up_proj):
@@ -43,6 +297,30 @@
         axis=1,
     )
     return lax.psum(home_proj, ("mp", "sub")).astype(jnp.bfloat16)
+
+
+def plain_projections(out_grad, gate_pre, up_pre, down_weight, proj_hidden, proj_gate, proj_up):
+    pieces = gate_pre.shape[1] // lax.axis_size("groups")
+    full_grads = lax.all_gather(out_grad, ("mp", "sub"), axis=1, tiled=True)
+    mine = lax.dynamic_slice_in_dim(down_weight, lax.axis_index("groups") * pieces, pieces, 0)
+    weight_part = lax.all_gather(mine, "dp", axis=1, tiled=True)
+    weight = lax.all_gather(weight_part, "groups", axis=0, tiled=True)
+    hidden_grad = lax.dot_general(
+        full_grads, weight, (((1,), (1,)), ((), ())), preferred_element_type=jnp.float32
+    )
+    gate_val = gate_pre.astype(jnp.float32)
+    up_val = up_pre.astype(jnp.float32)
+    sigmoid_gate = jax.nn.sigmoid(gate_val)
+    hidden = (gate_val * sigmoid_gate * up_val).astype(jnp.bfloat16)
+    gate_grad = (
+        hidden_grad * up_val * sigmoid_gate * (1.0 + gate_val * (1.0 - sigmoid_gate))
+    ).astype(jnp.bfloat16)
+    up_grad = (hidden_grad * gate_val * sigmoid_gate).astype(jnp.bfloat16)
+    return (
+        jnp.dot(hidden, proj_hidden, preferred_element_type=jnp.float32),
+        jnp.dot(gate_grad, proj_gate, preferred_element_type=jnp.float32),
+        jnp.dot(up_grad, proj_up, preferred_element_type=jnp.float32),
+    )
 
 
 def body(
@@ -58,27 +336,27 @@
     proj_gate,
     proj_up,
 ):
-    ff_cols = gate_pre.shape[1]
-    half = ff_cols // 2
-    full_grads = lax.all_gather(out_grad, ("mp", "sub"), axis=1, tiled=True)
-    mine = lax.dynamic_slice_in_dim(down_weight, lax.axis_index("groups") * half, half, 0)
-    weight_half = lax.all_gather(mine, "dp", axis=1, tiled=True)
-    weight = lax.all_gather(weight_half, "groups", axis=0, tiled=True)
     home_proj = home_projections(layer_input, out_grad, proj_input, proj_output)
-    hidden_grad = lax.dot_general(
-        full_grads, weight, (((1,), (1,)), ((), ())), preferred_element_type=jnp.float32
-    )
-    gate_val = gate_pre.astype(jnp.float32)
-    up_val = up_pre.astype(jnp.float32)
-    sigmoid_gate = jax.nn.sigmoid(gate_val)
-    hidden = (gate_val * sigmoid_gate * up_val).astype(jnp.bfloat16)
-    gate_grad = (
-        hidden_grad * up_val * sigmoid_gate * (1.0 + gate_val * (1.0 - sigmoid_gate))
-    ).astype(jnp.bfloat16)
-    up_grad = (hidden_grad * gate_val * sigmoid_gate).astype(jnp.bfloat16)
-    hidden_proj = jnp.dot(hidden, proj_hidden, preferred_element_type=jnp.float32)
-    gate_proj = jnp.dot(gate_grad, proj_gate, preferred_element_type=jnp.float32)
-    up_proj = jnp.dot(up_grad, proj_up, preferred_element_type=jnp.float32)
+    shards = lax.axis_size("dp")
+    feature_shards = lax.axis_size("mp") * lax.axis_size("sub")
+    even = gate_pre.shape[1] % (2 * CHUNK) == 0 and lax.axis_size("groups") == 2
+    if even and shards == feature_shards:
+        hidden_proj, gate_proj, up_proj = gathered_projections(
+            shards,
+            feature_shards,
+            lax.axis_size("sub"),
+            out_grad,
+            gate_pre,
+            up_pre,
+            down_weight,
+            proj_hidden,
+            proj_gate,
+            proj_up,
+        )
+    else:
+        hidden_proj, gate_proj, up_proj = plain_projections(
+            out_grad, gate_pre, up_pre, down_weight, proj_hidden, proj_gate, proj_up
+        )
     return example_sums(example_blocks, home_proj, hidden_proj, gate_proj, up_proj)
 
 

time: 757 us -> 377 us (0.50)
  waiting for transfers between devices: 669 us -> 57.7 us
  Pallas kernels: 0 us -> 272 us
  matrix products: 41.2 us -> 4.08 us
    all_gather x3 -> x0, waiting for transfers between devices: 609 us -> none  [the longest x1 344 us: body(): weight = lax.all_gather(weight_half, 'groups', axis=0, tiled=True)]
    pallas_call x0 -> x1, Pallas kernels: none -> 272 us  [gathered_projections(): pl.pallas_call(functools.partial(gather_kernel, shards, feature_shards, c...]
    dot_general x4 -> x0, matrix products: 39 us -> none  [the longest x1 24.5 us: body(): lax.dot_general(full_grads, weight, (((1,), (1,)), ((), ())), preferred_e...]
    unnamed x5 -> x2, waiting for transfers between devices: 59.3 us -> 57.7 us
  transfers between devices with their start and end apart: 4 -> 1, of which waited for: 4 -> 1; matrix products, arithmetic and copies ran while one was open for 1% -> 0% of each run, Pallas kernels for 0% -> 0%
where the time goes in v1:
time: 377 us
  Pallas kernels  272 us (72%)
  waiting for transfers between devices  57.7 us (15%)
  blocking collectives  16.5 us (4%)
  between operations  13.5 us (4%)
  local copies, waits for them, and re-layouts  12 us (3%)
  matrix products  4.08 us (1%)
    pallas_call x1, Pallas kernels, gathered_projections(): pl.pallas_call(functools.partial(gather_kernel, shards, feature_shards, c...  272 us
    unnamed x2, waiting for transfers between devices  57.7 us
    psum x1, blocking collectives, home_projections(): return lax.psum(home_proj, ('mp', 'sub')).astype(jnp.bfloat16)  16.5 us
    unnamed x17, local copies, waits for them, and re-layouts  10.4 us
  transfers between devices with their start and end apart: 1, of which 1 were waited for; matrix products, arithmetic and copies ran while one was open for 0% of the time, Pallas kernels for 0%

profile of v1, /device:TPU:0, one launch (start us, length us, event | category | flops | bytes accessed | tf_op | source)
XLA Modules:
  0.0 377.0 jit_solution(17016861607027340238)
XLA Ops:
  6.5 0.0 copy-start
  6.5 0.0 copy-start.1
  6.5 0.0 copy-start.5
  6.5 0.0 reduce-scatter.4.cloned.1.call-start
  6.5 1.0 reduce-window.8
  7.5 0.1 convert_reduce_fusion
  7.6 0.2 copy-done
  7.8 1.4 fusion.12
  9.2 0.0 copy-done.1
  9.2 0.0 copy-done.5
  9.2 0.0 copy-start.2
  9.2 0.5 fusion.13
  9.7 0.0 copy-start.3
  9.7 16.5 %all-reduce.1 = bf16[528,128]{0,1:T(8,128)(2,1)S(1)} all-reduce(f32[528,128]{0,1:T(8,128)S(1)} %pad_maximum_fusion), channel_id=1, replica_groups=mesh['groups'=2,'dp'=4,'mp'=2,'sub'=2] {'mp','sub'}, use_global_device_ids=true, to_apply=%region_2.3 | all-reduce | flops 67584 | bytes 405504 | tf_op jit(solution)/shard_map/psum | solution.py:299
  26.3 0.0 copy-done.2
  26.3 0.0 copy-start.4
  26.3 1.2 copy.26.proj_hidden_ref
  27.6 0.0 copy-done.3
  27.6 1.3 copy.27.proj_gate_ref
  28.9 0.0 copy-done.4
  28.9 1.2 copy.28.proj_up_ref
  30.1 272.0 %shard_map.109 = (f32[528,64]{1,0:T(8,128)}, f32[528,64]{1,0:T(8,128)}, f32[528,64]{1,0:T(8,128)}) custom-call(bf16[528,1024]{1,0:T(8,128)(2,1)} %grads_ref.1, bf16[528,3584]{1,0:T(8,128)(2,1)} %gate_ref.1, bf16[528,3584]{1,0:T(8,128)(2,1)} %up_ref.1, bf16[3584,1024]{1,0:T(8,128)(2,1)} %weight_ref.1, bf16[3584,64]{1,0:T(8,128)(2,1)} %copy.26.proj_hidden_ref, ...), custom_call_target="tpu_custom_call" | custom-call | flops 16228810752 | bytes 36929536 | tf_op jit(solution)/shard_map/pallas_call | solution.py:239
  302.1 1.1 copy.29
  303.2 1.8 fusion
  305.0 0.1 fusion.11
  305.1 0.1 reshape.68
  305.2 0.1 reshape.69
  305.4 0.4 fusion.7
  305.8 0.1 reshape_reshape.3
  306.0 4.0 %copy.32 = f32[4,12288]{0,1:T(8,128)} copy(f32[4,12288]{1,0:T(4,128)S(1)} %pad_maximum_fusion.1) | data formatting | bytes 393216
  310.0 0.0 reduce-scatter.4.cloned.1.call-update
  310.0 57.7 %reduce-scatter.4.cloned.1.call-done = f32[3072,4]{1,0:T(8,128)} async-done(((f32[12288,4]{1,0:T(8,128)}), f32[3072,4]{1,0:T(8,128)}) %reduce-scatter.4.cloned.1.call-update) | async-done | bytes 49168
  367.7 2.5 copy.33
  (6 shorter events, 0.1 us)
Async XLA Ops:
  6.5 1.3 copy-start
  6.5 2.6 copy-start.1
  6.5 2.7 copy-start.5
  6.5 361.1 %reduce-scatter.4.cloned.1.call-start = ((), (), s32[]{:S(2)}) async-start(), calls=%async_computation.1 | async-start | bytes 7864320
  9.2 17.1 %copy-start.2 = (bf16[3584,64]{0,1:T(8,128)(2,1)S(1)}, bf16[3584,64]{0,1:T(8,128)(2,1)}, u32[]{:S(2)}) copy-start(bf16[3584,64]{0,1:T(8,128)(2,1)} %param.19) | copy-start | bytes 1376260
  9.7 17.8 %copy-start.3 = (bf16[3584,64]{0,1:T(8,128)(2,1)S(1)}, bf16[3584,64]{0,1:T(8,128)(2,1)}, u32[]{:S(2)}) copy-start(bf16[3584,64]{0,1:T(8,128)(2,1)} %param.20) | copy-start | bytes 1376260
  26.3 2.5 copy-start.4
Sparse Core Ops, SparseCore 0:
  310.1 57.5 reduce-scatter.3

commit v2 on v1

--- a/solution.py
+++ b/solution.py
@@ -24,9 +24,17 @@
     proj_hidden_ref,
     proj_gate_ref,
     proj_up_ref,
+    inputs_ref,
+    proj_input_ref,
+    proj_output_ref,
+    selector_ref,
+    out_ref,
     hidden_out,
     gate_out,
     up_out,
+    home_parts,
+    sums,
+    arrived,
     weights,
     grads,
     grad_send,
@@ -37,6 +45,10 @@
     recv_sem,
     group_send,
     group_recv,
+    home_send,
+    home_recv,
+    sums_send,
+    sums_recv,
 ):
     group = lax.axis_index("groups")
     here = lax.axis_index("dp")
@@ -54,6 +66,31 @@
             dst_ref=grads.at[origin],
             send_sem=grad_send.at[to],
             recv_sem=grad_recv.at[origin],
+            device_id={"mp": to // cores, "sub": to % cores},
+            device_id_type=MESH,
+        )
+
+    def home_copy(to, origin):
+        return pltpu.make_async_remote_copy(
+            src_ref=home_parts.at[feature],
+            dst_ref=home_parts.at[origin],
+            send_sem=home_send.at[to],
+            recv_sem=home_recv.at[origin],
+            device_id={"mp": to // cores, "sub": to % cores},
+            device_id_type=MESH,
+        )
+
+    share = arrived.shape[2]
+
+    def share_of(at):
+        return pl.ds(pl.multiple_of(at * share, 8), share)
+
+    def sums_copy(to, origin):
+        return pltpu.make_async_remote_copy(
+            src_ref=sums.at[:, share_of(to), :],
+            dst_ref=arrived.at[origin],
+            send_sem=sums_send.at[to],
+            recv_sem=sums_recv.at[origin],
             device_id={"mp": to // cores, "sub": to % cores},
             device_id_type=MESH,
         )
@@ -126,6 +163,22 @@
     local_grads.start()
     local_weight = pltpu.make_async_copy(weight_ref, weights.at[here], local_sem.at[1])
     local_weight.start()
+    rank_dim = proj_input_ref.shape[0]
+
+    def turned_dot(left, right):
+        return lax.dot_general(
+            left, right, (((1,), (1,)), ((), ())), preferred_element_type=jnp.float32
+        )
+
+    home_parts[feature] = jnp.concatenate(
+        [
+            turned_dot(inputs_ref[...], proj_input_ref[...]),
+            turned_dot(grads_ref[...], proj_output_ref[...]),
+        ],
+        axis=1,
+    )
+    for step in range(1, feature_shards):
+        home_copy(lax.rem(feature + step, feature_shards), feature).start()
     hidden_out[...] = jnp.zeros_like(hidden_out)
     gate_out[...] = jnp.zeros_like(gate_out)
     up_out[...] = jnp.zeros_like(up_out)
@@ -160,13 +213,9 @@
             hidden_grad * up_val * sigmoid_gate * (1.0 + gate_val * (1.0 - sigmoid_gate))
         ).astype(jnp.bfloat16)
         up_grad = (hidden_grad * silu_gate).astype(jnp.bfloat16)
-        hidden_out[...] += jnp.dot(
-            hidden, proj_hidden_ref[span, :], preferred_element_type=jnp.float32
-        )
-        gate_out[...] += jnp.dot(
-            gate_grad, proj_gate_ref[span, :], preferred_element_type=jnp.float32
-        )
-        up_out[...] += jnp.dot(up_grad, proj_up_ref[span, :], preferred_element_type=jnp.float32)
+        hidden_out[...] += turned_dot(hidden, proj_hidden_ref[:, span])
+        gate_out[...] += turned_dot(gate_grad, proj_gate_ref[:, span])
+        up_out[...] += turned_dot(up_grad, proj_up_ref[:, span])
 
     def tick(at, carry):
         @pl.when(at + 1 < chunks)
@@ -204,6 +253,42 @@
         return carry
 
     lax.fori_loop(0, chunks + shards, tick, 0)
+
+    for step in range(1, feature_shards):
+        origin = lax.rem(feature + step, feature_shards)
+        home_copy(origin, origin).wait_recv()
+        home_copy(origin, feature).wait_send()
+    home = home_parts[0]
+    for origin in range(1, feature_shards):
+        home += home_parts[origin]
+    home = home.astype(jnp.bfloat16).astype(jnp.float32)
+    input_side, output_side = home[:, :rank_dim], home[:, rank_dim:]
+    num_examples = sums.shape[0]
+
+    def outer(left, right):
+        return lax.dot_general(
+            left,
+            right,
+            (((0,), (0,)), ((), ())),
+            precision=lax.Precision.HIGHEST,
+            preferred_element_type=jnp.float32,
+        )
+
+    for example in range(num_examples):
+        chosen = selector_ref[:, example : example + 1]
+        sums[example, :rank_dim, :] = outer(hidden_out[...] * chosen, output_side)
+        left = input_side * chosen
+        sums[example, rank_dim : 2 * rank_dim, :] = outer(left, gate_out[...])
+        sums[example, 2 * rank_dim :, :] = outer(left, up_out[...])
+    for step in range(1, feature_shards):
+        sums_copy(lax.rem(feature + step, feature_shards), feature).start()
+    out_ref[...] = sums[:, share_of(feature), :]
+    for step in range(1, feature_shards):
+        origin = lax.rem(feature + step, feature_shards)
+        sums_copy(origin, origin).wait_recv()
+        out_ref[...] += arrived[origin]
+    for step in range(1, feature_shards):
+        sums_copy(lax.rem(feature + step, feature_shards), feature).wait_send()
 
     for step in range(1, feature_shards):
         grad_copy(lax.rem(feature + step, feature_shards), feature).wait_send()
@@ -227,49 +312,71 @@
     lax.fori_loop(0, chunks, drain, 0)
 
 
-def gathered_projections(
-    shards, feature_shards, cores, out_grad, gate_pre, up_pre, down_weight, proj_hidden, proj_gate, proj_up
+def gathered_sums(
+    shards, feature_shards, cores, example_blocks, layer_input, out_grad, gate_pre, up_pre, down_weight, projections
 ):
     rows, columns = out_grad.shape
     ff_cols = gate_pre.shape[1]
-    rank_dim = proj_hidden.shape[1]
+    rank_dim = projections[0].shape[1]
+    num_examples = example_blocks.shape[0]
     chunks = ff_cols // (2 * CHUNK)
+    share = 3 * rank_dim // feature_shards
     in_vmem = pl.BlockSpec(memory_space=pltpu.VMEM)
     full = columns * feature_shards
-    return pl.pallas_call(
+    turned = [projection.T for projection in projections]
+    summed = pl.pallas_call(
         functools.partial(gather_kernel, shards, feature_shards, cores, chunks),
-        out_shape=[jax.ShapeDtypeStruct((rows, rank_dim), jnp.float32)] * 3,
-        in_specs=[in_vmem] * 3 + [pl.BlockSpec(memory_space=pl.ANY)] + [in_vmem] * 3,
-        out_specs=[in_vmem] * 3,
-        scratch_shapes=[
+        out_shape=jax.ShapeDtypeStruct((num_examples, share, rank_dim), jnp.float32),
+        in_specs=[in_vmem] * 3 + [pl.BlockSpec(memory_space=pl.ANY)] + [in_vmem] * 7,
+        out_specs=in_vmem,
+        scratch_shapes=[pltpu.VMEM((rows, rank_dim), jnp.float32)] * 3
+        + [
+            pltpu.VMEM((feature_shards, rows, 2 * rank_dim), jnp.float32),
+            pltpu.VMEM((num_examples, 3 * rank_dim, rank_dim), jnp.float32),
+            pltpu.VMEM((feature_shards, num_examples, share, rank_dim), jnp.float32),
             pltpu.VMEM((shards, ff_cols, columns), jnp.bfloat16),
             pltpu.VMEM((feature_shards, rows, columns), jnp.bfloat16),
             pltpu.SemaphoreType.DMA((feature_shards,)),
             pltpu.SemaphoreType.DMA((feature_shards,)),
             pltpu.SemaphoreType.DMA((2,)),
         ]
-        + [pltpu.SemaphoreType.DMA((shards, chunks))] * 5,
+        + [pltpu.SemaphoreType.DMA((shards, chunks))] * 5
+        + [pltpu.SemaphoreType.DMA((feature_shards,))] * 4,
         compiler_params=pltpu.CompilerParams(
-            collective_id=0, has_side_effects=True, vmem_limit_bytes=60 * 2**20
+            collective_id=0, has_side_effects=True, vmem_limit_bytes=62 * 2**20
         ),
         cost_estimate=pl.CostEstimate(
             flops=2 * rows * ff_cols * (full + 3 * rank_dim),
             bytes_accessed=2 * ff_cols * (2 * rows + full),
             transcendentals=rows * ff_cols,
         ),
-    )(out_grad, gate_pre, up_pre, down_weight, proj_hidden, proj_gate, proj_up)
+    )(
+        out_grad,
+        gate_pre,
+        up_pre,
+        down_weight,
+        *turned[2:],
+        layer_input,
+        *turned[:2],
+        row_selector(example_blocks, rows),
+    )
+    return summed.reshape(num_examples, share * rank_dim)
+
+
+def row_selector(example_blocks, rows):
+    num_examples = example_blocks.shape[0]
+    labels = jnp.arange(num_examples, dtype=jnp.int32)
+    earlier = (labels[:, None] <= labels[None, :]).astype(jnp.int32)
+    block_ends = jnp.sum(example_blocks[:, None] * earlier, axis=0) * BLK
+    row_ids = jnp.arange(rows, dtype=jnp.int32)[:, None]
+    inside = (row_ids < block_ends[None, :]) & (row_ids >= (block_ends - example_blocks * BLK)[None, :])
+    return inside.astype(jnp.float32)
 
 
 def example_sums(example_blocks, home_proj, hidden_proj, gate_proj, up_proj):
     rows, rank_dim = hidden_proj.shape
     num_examples = example_blocks.shape[0]
-    block_ends = jnp.cumsum(example_blocks) * BLK
-    row_ids = jnp.arange(rows, dtype=jnp.int32)
-    row_example = jnp.sum(
-        (row_ids[:, None] >= block_ends[None, :]).astype(jnp.int32), axis=1, dtype=jnp.int32
-    )
-    labels = jnp.arange(num_examples, dtype=jnp.int32)
-    selector = (row_example[:, None] == labels[None, :]).astype(jnp.float32)
+    selector = row_selector(example_blocks, rows)
     input_side = home_proj[:, :rank_dim].astype(jnp.float32)
     output_side = home_proj[:, rank_dim:].astype(jnp.float32)
 
@@ -336,27 +443,27 @@
     proj_gate,
     proj_up,
 ):
-    home_proj = home_projections(layer_input, out_grad, proj_input, proj_output)
     shards = lax.axis_size("dp")
     feature_shards = lax.axis_size("mp") * lax.axis_size("sub")
     even = gate_pre.shape[1] % (2 * CHUNK) == 0 and lax.axis_size("groups") == 2
+    even = even and (3 * proj_up.shape[1]) % (8 * feature_shards) == 0
     if even and shards == feature_shards:
-        hidden_proj, gate_proj, up_proj = gathered_projections(
+        return gathered_sums(
             shards,
             feature_shards,
             lax.axis_size("sub"),
+            example_blocks,
+            layer_input,
             out_grad,
             gate_pre,
             up_pre,
             down_weight,
-            proj_hidden,
-            proj_gate,
-            proj_up,
-        )
-    else:
-        hidden_proj, gate_proj, up_proj = plain_projections(
-            out_grad, gate_pre, up_pre, down_weight, proj_hidden, proj_gate, proj_up
-        )
+            (proj_input, proj_output, proj_hidden, proj_gate, proj_up),
+        )
+    home_proj = home_projections(layer_input, out_grad, proj_input, proj_output)
+    hidden_proj, gate_proj, up_proj = plain_projections(
+        out_grad, gate_pre, up_pre, down_weight, proj_hidden, proj_gate, proj_up
+    )
     return example_sums(example_blocks, home_proj, hidden_proj, gate_proj, up_proj)
 
 

time: 377 us -> 284 us (0.75)
  waiting for transfers between devices: 57.7 us -> 0 us
  blocking collectives: 16.5 us -> 0 us
  between operations: 13.5 us -> 0.01 us
  local copies, waits for them, and re-layouts: 12 us -> 1.61 us
  Pallas kernels: 272 us -> 280 us
  matrix products: 4.08 us -> 0 us
    unnamed x2 -> x0, waiting for transfers between devices: 57.7 us -> none
    psum x1 -> x0, blocking collectives: 16.5 us -> none  [home_projections(): return lax.psum(home_proj, ('mp', 'sub')).astype(jnp.bfloat16)]
    unnamed x17 -> x0, local copies, waits for them, and re-layouts: 10.4 us -> none
    pallas_call x1, Pallas kernels: 272 us -> 280 us  [gathered_sums(): pl.pallas_call(functools.partial(gather_kernel, shards, feature_shards, c...]
    dot_general x4 -> x0, matrix products: 4.08 us -> none  [the longest x2 2.22 us: outer(): lax.dot_general(left, right, (((0,), (0,)), ((), ())), precision=lax.Prec...]
  transfers between devices with their start and end apart: 1 -> 0, of which waited for: 1 -> 0; matrix products, arithmetic and copies ran while one was open for 0% -> 0% of each run, Pallas kernels for 0% -> 0%
where the time goes in v2:
time: 284 us
  Pallas kernels  280 us (99%)
    pallas_call x1, Pallas kernels, gathered_sums(): pl.pallas_call(functools.partial(gather_kernel, shards, feature_shards, c...  280 us

profile of v2, /device:TPU:0, one launch (start us, length us, event | category | flops | bytes accessed | tf_op | source)
XLA Modules:
  0.0 283.6 jit_solution(12538998546796386114)
XLA Ops:
  0.0 0.7 select_reduce_fusion
  0.7 0.7 multiply_subtract_fusion
  1.4 0.8 fusion.1.selector_ref
  2.2 279.9 %shard_map.109 = f32[4,48,64]{2,1,0:T(8,128)} custom-call(bf16[528,1024]{1,0:T(8,128)(2,1)} %grads_ref.1, bf16[528,3584]{1,0:T(8,128)(2,1)} %gate_ref.1, bf16[528,3584]{1,0:T(8,128)(2,1)} %up_ref.1, bf16[3584,1024]{1,0:T(8,128)(2,1)} %weight_ref.1, bf16[64,3584]{1,0:T(8,128)(2,1)} %bitcast.5, bf16[64,3584]{1,0:T(8,128)(2,1)} %bitcast.6, ...), custom_call_target="tpu_custom_call" | custom-call | flops 16228810752 | bytes 36929536 | tf_op jit(solution)/shard_map/pallas_call | solution.py:327
  282.0 1.6 reshape.8

commit v3 on v2

--- a/solution.py
+++ b/solution.py
@@ -157,6 +157,7 @@
             line_copy(own, here, chunk, here - 1, send_left).start()
 
     send_own(0)
+    send_own(1)
     for step in range(1, feature_shards):
         grad_copy(lax.rem(feature + step, feature_shards), feature).start()
     local_grads = pltpu.make_async_copy(grads_ref, grads.at[feature], local_sem.at[0])
@@ -218,9 +219,9 @@
         up_out[...] += turned_dot(up_grad, proj_up_ref[:, span])
 
     def tick(at, carry):
-        @pl.when(at + 1 < chunks)
-        def _():
-            send_own(at + 1)
+        @pl.when(at + 2 < chunks)
+        def _():
+            send_own(at + 2)
 
         for step in range(1, shards):
             chunk = at - step
@@ -446,7 +447,7 @@
     shards = lax.axis_size("dp")
     feature_shards = lax.axis_size("mp") * lax.axis_size("sub")
     even = gate_pre.shape[1] % (2 * CHUNK) == 0 and lax.axis_size("groups") == 2
-    even = even and (3 * proj_up.shape[1]) % (8 * feature_shards) == 0
+    even = even and gate_pre.shape[1] >= 4 * CHUNK and (3 * proj_up.shape[1]) % (8 * feature_shards) == 0
     if even and shards == feature_shards:
         return gathered_sums(
             shards,

time: 284 us -> 295 us (1.039)
  Pallas kernels: 280 us -> 291 us
    pallas_call x1, Pallas kernels: 280 us -> 291 us  [gathered_sums(): pl.pallas_call(functools.partial(gather_kernel, shards, feature_shards, c...]
where the time goes in v3:
time: 295 us
  Pallas kernels  291 us (99%)
    pallas_call x1, Pallas kernels, gathered_sums(): pl.pallas_call(functools.partial(gather_kernel, shards, feature_shards, c...  291 us

profile of v3, /device:TPU:0, one launch (start us, length us, event | category | flops | bytes accessed | tf_op | source)
XLA Modules:
  0.0 294.9 jit_solution(6268482314773817015)
XLA Ops:
  0.0 0.7 select_reduce_fusion
  0.7 0.7 multiply_subtract_fusion
  1.4 0.8 fusion.1.selector_ref
  2.2 291.1 %shard_map.109 = f32[4,48,64]{2,1,0:T(8,128)} custom-call(bf16[528,1024]{1,0:T(8,128)(2,1)} %grads_ref.1, bf16[528,3584]{1,0:T(8,128)(2,1)} %gate_ref.1, bf16[528,3584]{1,0:T(8,128)(2,1)} %up_ref.1, bf16[3584,1024]{1,0:T(8,128)(2,1)} %weight_ref.1, bf16[64,3584]{1,0:T(8,128)(2,1)} %bitcast.5, bf16[64,3584]{1,0:T(8,128)(2,1)} %bitcast.6, ...), custom_call_target="tpu_custom_call" | custom-call | flops 16228810752 | bytes 36929536 | tf_op jit(solution)/shard_map/pallas_call | solution.py:328
  293.3 1.6 reshape.8
